TPU v7x, 32 devices: a whole 2x2x4 slice. The times are simulated.
32 devices in a mesh: grid: 16 (over z, x, core), layer: 2 (over y).
Axes of the slice: x: 2, y: 2, z: 4, core: 2. Of those that a mesh axis runs over, the one named last changes fastest.
Arguments:
- x_tiles: bfloat16 [16, 512, 512], P('grid'), may hold values from -1.03 to 1.03, as said below
- pattern: int32 [16, 8, 8], P('grid'), may hold values from 0 to 1, as said below
Outputs:
- signed: bfloat16 [16, 128, 512], P('grid', 'layer')
Inputs may be any that keep to these rules, and one draw needn't show every extreme that they name: `x_tiles`: tile (j, i) is the transpose of tile (i, j). symmetric: the block pattern of the whole matrix is its own transpose, and every diagonal block is kept.
All inputs are finite; a program needn't handle non-finite values.
Results may differ from a plain program's by a relative error of at most 0.013.
Values may be sent and summed in bfloat16 or wider, within the bound.
A program may use at most 64 MiB of HBM per device.

v0:
```python
import math

import jax
import jax.numpy as jnp
from jax import lax
from jax.sharding import PartitionSpec as P

SLAB = 128


def from_partner(block, axis, apart):
    count = lax.axis_size(axis)
    route = []
    for low in range(count):
        high = low | 1 << apart
        if high != low and high < count:
            route += [(low, high), (high, low)]
    return lax.ppermute(block, axis, route)


def row_move(tile, level):
    return from_partner(tile, "grid", level)


def col_move(tile, level):
    return from_partner(tile, "grid", level)


def tile_product(left, right):
    occupied = jnp.any(left != 0) & jnp.any(right != 0)

    def multiply(operands):
        return jnp.dot(operands[0], operands[1], preferred_element_type=jnp.float32)

    def nothing(operands):
        return jnp.zeros((operands[0].shape[0], operands[1].shape[1]), jnp.float32)

    return lax.cond(occupied, multiply, nothing, (left, right))


def lowest_bit(number):
    level = 0
    while number >> level & 1 == 0:
        level = level + 1
    return level


def gray_flips(turns):
    flips = []
    for inner in range(min(turns, 8)):
        if inner > 0:
            flips.append(lowest_bit(inner))
    return flips


def align_left(left, amount, bit_count):
    for level in range(bit_count):
        moved = row_move(left, level)
        left = jnp.where(amount >> level & 1 == 1, moved, left)
    return left


def walk(left, right, flips, bit_count):
    total = tile_product(left, right)
    for level in flips:
        left = row_move(left, level)
        right = col_move(right, level + bit_count)
        total = total + tile_product(left, right)
    return (total, right)


def shards(x_tiles, pattern):
    side = math.isqrt(lax.axis_size("grid"))
    bit_count = side.bit_length() - 1
    layers = lax.axis_size("layer")
    position = lax.axis_index("grid")
    row_index = position // side
    column = position % side
    layer_index = lax.axis_index("layer")
    blocks = pattern.shape[1]
    width = x_tiles.shape[1]
    span = width // blocks
    mask = jnp.broadcast_to(pattern[0][:, None, :, None], (blocks, span, blocks, span))
    mask = mask.reshape(width, width).astype(jnp.bfloat16)
    matrix = x_tiles[0] * mask
    slab = matrix[:SLAB]
    share = SLAB // layers
    own = lax.dynamic_slice_in_dim(slab, layer_index * share, share, 0)
    turns = side // layers
    start = layer_index * turns
    flips = gray_flips(turns)
    finish = start ^ turns // 2
    left = align_left(slab, row_index ^ start, bit_count)
    right = matrix
    right_amount = column ^ start
    for level in range(bit_count):
        moved = col_move(right, level + bit_count)
        right = jnp.where(right_amount >> level & 1 == 1, moved, right)
    partial_value, ending = walk(left, right, flips, bit_count)
    squared = lax.psum(partial_value.astype(jnp.bfloat16), "layer")
    second_left = align_left(squared, row_index ^ finish, bit_count)
    partial_next, unused = walk(second_left, ending, flips[::-1], bit_count)
    cubed = lax.psum_scatter(
        partial_next.astype(jnp.bfloat16), "layer", scatter_dimension=0, tiled=True
    ).astype(jnp.float32)
    signed = (1.5 * own.astype(jnp.float32) - 0.5 * cubed).astype(jnp.bfloat16)
    return signed[None]


def solution(mesh):
    in_specs = (P("grid", None, None), P("grid", None, None))
    out_specs = P("grid", "layer", None)
    return jax.shard_map(shards, mesh=mesh, in_specs=in_specs, out_specs=out_specs, check_vma=False)
```

profile of v0, /device:TPU:0, one launch (start us, length us, event | category | flops | bytes accessed | tf_op | source)
XLA Modules:
  0.0 129.4 jit_solution(9939733951687233370)
XLA Ops:
  6.5 0.7 convert_bitcast_fusion
  7.2 0.2 broadcast_in_dim.8
  7.4 0.0 copy-start
  7.5 0.6 convert_element_type.39
  8.1 0.4 copy-done
  8.5 0.1 bitcast_multiply_fusion
  8.5 3.1 %collective-permute-start.2 = (bf16[512,512]{1,0:T(8,128)(2,1)S(1)}, bf16[512,512]{1,0:T(8,128)(2,1)S(1)}, u32[]{:S(2)}, u32[]{:S(2)}) collective-permute-start(bf16[512,512]{1,0:T(8,128)(2,1)S(1)} %bitcast_multiply_fusion), channel_id=1, source_target_pairs={{0,8},{8,0},{2,10},{10,2},{4,12},{12,4},{6,14},{14,6},{16,24},{24,... | collective-permute-start | bytes 1572872 | tf_op jit(solution)/shard_map/ppermute | solution.py:18
  11.6 11.9 %collective-permute-done.2 = bf16[512,512]{1,0:T(8,128)(2,1)S(1)} collective-permute-done((bf16[512,512]{1,0:T(8,128)(2,1)S(1)}, bf16[512,512]{1,0:T(8,128)(2,1)S(1)}, u32[]{:S(2)}, u32[]{:S(2)}) %collective-permute-start.2) | collective-permute-done | bytes 524320 | tf_op jit(solution)/shard_map/ppermute | solution.py:18
  23.6 0.1 broadcast_select_fusion
  23.6 2.8 %collective-permute-start.3 = (bf16[512,512]{1,0:T(8,128)(2,1)S(1)}, bf16[512,512]{1,0:T(8,128)(2,1)S(1)}, u32[]{:S(2)}, u32[]{:S(2)}) collective-permute-start(bf16[512,512]{1,0:T(8,128)(2,1)S(1)} %broadcast_select_fusion), channel_id=1, source_target_pairs={{0,16},{16,0},{2,18},{18,2},{4,20},{20,4},{6,22},{22,6},{8,24},{24... | collective-permute-start | bytes 1572872 | tf_op jit(solution)/shard_map/ppermute | solution.py:18
  26.4 0.1 collective-permute-start
  26.5 1.3 %collective-permute-done = bf16[128,512]{1,0:T(8,128)(2,1)S(1)} collective-permute-done((bf16[128,512]{1,0:T(8,128)(2,1)S(1)}, bf16[128,512]{1,0:T(8,128)(2,1)S(1)}, u32[]{:S(2)}, u32[]{:S(2)}) %collective-permute-start) | collective-permute-done | bytes 131104 | tf_op jit(solution)/shard_map/ppermute | solution.py:18
  27.9 1.6 %collective-permute-start.1 = (bf16[128,512]{1,0:T(8,128)(2,1)S(1)}, bf16[128,512]{1,0:T(8,128)(2,1)S(1)}, u32[]{:S(2)}, u32[]{:S(2)}) collective-permute-start(bf16[128,512]{1,0:T(8,128)(2,1)S(1)} %broadcast_select_fusion.2), channel_id=1, source_target_pairs={{0,4},{4,0},{2,6},{6,2},{8,12},{12,8},{10,14},{14,10},{16,20},{20,... | collective-permute-start | bytes 393224 | tf_op jit(solution)/shard_map/ppermute | solution.py:18
  29.4 19.5 %collective-permute-done.3 = bf16[512,512]{1,0:T(8,128)(2,1)S(1)} collective-permute-done((bf16[512,512]{1,0:T(8,128)(2,1)S(1)}, bf16[512,512]{1,0:T(8,128)(2,1)S(1)}, u32[]{:S(2)}, u32[]{:S(2)}) %collective-permute-start.3) | collective-permute-done | bytes 524320 | tf_op jit(solution)/shard_map/ppermute | solution.py:18
  48.9 1.6 %compare_reduce_fusion.2 = (pred[]{:T(512)}, bf16[512,512]{1,0:T(8,128)(2,1)}) fusion(bf16[512,512]{1,0:T(8,128)(2,1)S(1)} %collective-permute-done.3, bf16[512,512]{1,0:T(8,128)(2,1)S(1)} %broadcast_select_fusion, pred[]{:T(512)S(6)} %eq.24), kind=kLoop, calls=%fused_computation.2 | loop fusion | flops 786431 | bytes 1572866 | tf_op jit(solution)/shard_map/reduce_or | solution.py:30
  50.5 0.5 collective-permute-start.5
  51.0 0.0 collective-permute-done.1
  51.0 0.7 compare_reduce_fusion.6
  51.7 0.0 collective-permute-start.4
  51.7 1.3 %collective-permute-done.4 = bf16[128,512]{1,0:T(8,128)(2,1)S(1)} collective-permute-done((bf16[128,512]{1,0:T(8,128)(2,1)S(1)}, bf16[128,512]{1,0:T(8,128)(2,1)S(1)}, u32[]{:S(2)}, u32[]{:S(2)}) %collective-permute-start.4) | collective-permute-done | bytes 131104 | tf_op jit(solution)/shard_map/ppermute | solution.py:18
  53.1 0.7 compare_reduce_fusion.5
  55.1 1.3 conditional.4
  55.1 1.3 fusion.1
  56.4 7.4 %collective-permute-done.5 = bf16[512,512]{1,0:T(8,128)(2,1)} collective-permute-done((bf16[512,512]{1,0:T(8,128)(2,1)}, bf16[512,512]{1,0:T(8,128)(2,1)}, u32[]{:S(2)}, u32[]{:S(2)}) %collective-permute-start.5) | collective-permute-done | bytes 524320 | tf_op jit(solution)/shard_map/ppermute | solution.py:18
  63.8 1.8 %compare_reduce_fusion.1 = pred[]{:T(512)} fusion(bf16[512,512]{1,0:T(8,128)(2,1)} %collective-permute-done.5), kind=kLoop, calls=%fused_computation.1 | loop fusion | flops 524287 | bytes 524289 | tf_op jit(solution)/shard_map/reduce_or | solution.py:30
  66.9 1.3 conditional.5
  66.9 1.3 fusion.2
  68.2 0.7 add_convert_fusion.1
  68.8 0.0 all-reduce.2.cloned.1.call-update
  68.9 0.0 reduce-scatter.2.cloned.1.call-start
  68.9 23.5 %all-reduce.2.cloned.1.call-done = bf16[128,512]{1,0:T(8,128)(2,1)} async-done(((bf16[128,512]{1,0:T(8,128)(2,1)}), bf16[128,512]{1,0:T(8,128)(2,1)}) %all-reduce.2.cloned.1.call-update) | async-done | bytes 131088 | tf_op jit(solution)/shard_map/psum | solution.py:100
  92.4 1.5 %collective-permute-start.9 = (bf16[512,512]{1,0:T(8,128)(2,1)}, bf16[512,512]{1,0:T(8,128)(2,1)S(1)}, u32[]{:S(2)}, u32[]{:S(2)}) collective-permute-start(bf16[512,512]{1,0:T(8,128)(2,1)} %collective-permute-done.5), channel_id=1, source_target_pairs={{0,8},{8,0},{2,10},{10,2},{4,12},{12,4},{6,14},{14,6},{16,24},{24,... | collective-permute-start | bytes 1572872 | tf_op jit(solution)/shard_map/ppermute | solution.py:18
  93.9 0.1 collective-permute-done.6
  93.9 1.5 %collective-permute-start.7 = (bf16[128,512]{1,0:T(8,128)(2,1)S(1)}, bf16[128,512]{1,0:T(8,128)(2,1)S(1)}, u32[]{:S(2)}, u32[]{:S(2)}) collective-permute-start(bf16[128,512]{1,0:T(8,128)(2,1)S(1)} %broadcast_select_fusion.4), channel_id=1, source_target_pairs={{0,4},{4,0},{2,6},{6,2},{8,12},{12,8},{10,14},{14,10},{16,20},{20,... | collective-permute-start | bytes 393224 | tf_op jit(solution)/shard_map/ppermute | solution.py:18
  95.5 4.1 %collective-permute-done.7 = bf16[128,512]{1,0:T(8,128)(2,1)S(1)} collective-permute-done((bf16[128,512]{1,0:T(8,128)(2,1)S(1)}, bf16[128,512]{1,0:T(8,128)(2,1)S(1)}, u32[]{:S(2)}, u32[]{:S(2)}) %collective-permute-start.7) | collective-permute-done | bytes 131104 | tf_op jit(solution)/shard_map/ppermute | solution.py:18
  99.6 1.4 %compare_reduce_fusion.4 = (pred[]{:T(512)}, bf16[128,512]{1,0:T(8,128)(2,1)}) fusion(bf16[128,512]{1,0:T(8,128)(2,1)S(1)} %collective-permute-done.7, bf16[128,512]{1,0:T(8,128)(2,1)S(1)} %broadcast_select_fusion.4, pred[]{:T(512)S(6)} %eq.20), kind=kLoop, calls=%fused_computation.9 | loop fusion | flops 196607 | bytes 393218 | tf_op jit(solution)/shard_map/reduce_or | solution.py:30
  102.2 0.1 collective-permute-start.8
  102.3 1.4 %conditional.6 = (f32[128,512]{1,0:T(8,128)S(1)}) conditional(s32[]{:T(128)} %convert_element_type.44, () %tuple.33, (bf16[128,512]{1,0:T(8,128)(2,1)}, bf16[512,512]{1,0:T(8,128)(2,1)}) %tuple.34), branch_computations={%region_10.11_spmd, %region_11.12_spmd} | conditional | flops 67108864 | bytes 917512 | solution.py:38
  102.3 1.3 %fusion.3 = f32[128,512]{1,0:T(8,128)S(1)} fusion(bf16[128,512]{1,0:T(8,128)(2,1)} %get-tuple-element.37, bf16[512,512]{1,0:T(8,128)(2,1)} %get-tuple-element.38), kind=kOutput, calls=%fused_computation.21 | convolution fusion | flops 67108864 | bytes 917504 | tf_op jit(solution)/shard_map/cond/branch_1_fun/dot_general | solution.py:33
  103.7 3.3 %collective-permute-done.9 = bf16[512,512]{1,0:T(8,128)(2,1)S(1)} collective-permute-done((bf16[512,512]{1,0:T(8,128)(2,1)}, bf16[512,512]{1,0:T(8,128)(2,1)S(1)}, u32[]{:S(2)}, u32[]{:S(2)}) %collective-permute-start.9) | collective-permute-done | bytes 524320 | tf_op jit(solution)/shard_map/ppermute | solution.py:18
  106.9 0.8 compare_reduce_fusion
  107.7 0.7 compare_reduce_fusion.3
  109.7 0.2 conditional.7
  109.7 0.2 fusion.4
  109.9 0.7 add_convert_fusion
  110.6 0.0 reduce-scatter.2.cloned.1.call-update
  110.6 10.4 %reduce-scatter.2.cloned.1.call-done = bf16[64,512]{1,0:T(8,128)(2,1)} async-done(((bf16[128,512]{1,0:T(8,128)(2,1)}), bf16[64,512]{1,0:T(8,128)(2,1)}) %reduce-scatter.2.cloned.1.call-update) | async-done | bytes 65552 | tf_op jit(solution)/shard_map/reduce_scatter | solution.py:103
  121.0 1.5 %fusion = bf16[1,64,512]{2,1,0:T(8,128)(2,1)} fusion(bf16[64,512]{1,0:T(8,128)(2,1)} %reduce-scatter.2.cloned.1.call-done, bf16[128,512]{1,0:T(8,128)(2,1)S(1)} %slice.4, s32[]{:T(128)S(6)} %select_n.54), kind=kLoop, calls=%fused_computation.17 | loop fusion | flops 196608 | bytes 196612 | tf_op jit(solution)/shard_map/broadcast_in_dim | solution.py:107
  (6 shorter events, 0.1 us)
Async XLA Ops:
  6.5 85.8 %all-reduce.2.cloned.1.call-start = ((), (), s32[]{:S(2)}) async-start(), calls=%async_computation.1 | async-start | bytes 262144 | tf_op jit(solution)/shard_map/psum | solution.py:100
  7.4 1.0 copy-start
  8.5 15.0 %collective-permute-start.2 = (bf16[512,512]{1,0:T(8,128)(2,1)S(1)}, bf16[512,512]{1,0:T(8,128)(2,1)S(1)}, u32[]{:S(2)}, u32[]{:S(2)}) collective-permute-start(bf16[512,512]{1,0:T(8,128)(2,1)S(1)} %bitcast_multiply_fusion), channel_id=1, source_target_pairs={{0,8},{8,0},{2,10},{10,2},{4,12},{12,4},{6,14},{14,6},{16,24},{24,... | collective-permute-start | bytes 1572872 | tf_op jit(solution)/shard_map/ppermute | solution.py:18
  23.6 25.3 %collective-permute-start.3 = (bf16[512,512]{1,0:T(8,128)(2,1)S(1)}, bf16[512,512]{1,0:T(8,128)(2,1)S(1)}, u32[]{:S(2)}, u32[]{:S(2)}) collective-permute-start(bf16[512,512]{1,0:T(8,128)(2,1)S(1)} %broadcast_select_fusion), channel_id=1, source_target_pairs={{0,16},{16,0},{2,18},{18,2},{4,20},{20,4},{6,22},{22,6},{8,24},{24... | collective-permute-start | bytes 1572872 | tf_op jit(solution)/shard_map/ppermute | solution.py:18
  26.4 1.4 %collective-permute-start = (bf16[128,512]{1,0:T(8,128)(2,1)S(1)}, bf16[128,512]{1,0:T(8,128)(2,1)S(1)}, u32[]{:S(2)}, u32[]{:S(2)}) collective-permute-start(bf16[128,512]{1,0:T(8,128)(2,1)S(1)} %slice.4), channel_id=1, source_target_pairs={{0,2},{2,0},{4,6},{6,4},{8,10},{10,8},{12,14},{14,12},{16,18},{18,... | collective-permute-start | bytes 393224 | tf_op jit(solution)/shard_map/ppermute | solution.py:18
  27.9 23.2 %collective-permute-start.1 = (bf16[128,512]{1,0:T(8,128)(2,1)S(1)}, bf16[128,512]{1,0:T(8,128)(2,1)S(1)}, u32[]{:S(2)}, u32[]{:S(2)}) collective-permute-start(bf16[128,512]{1,0:T(8,128)(2,1)S(1)} %broadcast_select_fusion.2), channel_id=1, source_target_pairs={{0,4},{4,0},{2,6},{6,2},{8,12},{12,8},{10,14},{14,10},{16,20},{20,... | collective-permute-start | bytes 393224 | tf_op jit(solution)/shard_map/ppermute | solution.py:18
  50.5 13.2 %collective-permute-start.5 = (bf16[512,512]{1,0:T(8,128)(2,1)}, bf16[512,512]{1,0:T(8,128)(2,1)}, u32[]{:S(2)}, u32[]{:S(2)}) collective-permute-start(bf16[512,512]{1,0:T(8,128)(2,1)} %get-tuple-element.44), channel_id=1, source_target_pairs={{0,8},{8,0},{2,10},{10,2},{4,12},{12,4},{6,14},{14,6},{16,24},{24,... | collective-permute-start | bytes 1572872 | tf_op jit(solution)/shard_map/ppermute | solution.py:18
  51.7 1.3 %collective-permute-start.4 = (bf16[128,512]{1,0:T(8,128)(2,1)S(1)}, bf16[128,512]{1,0:T(8,128)(2,1)S(1)}, u32[]{:S(2)}, u32[]{:S(2)}) collective-permute-start(bf16[128,512]{1,0:T(8,128)(2,1)S(1)} %get-tuple-element.46), channel_id=1, source_target_pairs={{0,2},{2,0},{4,6},{6,4},{8,10},{10,8},{12,14},{14,12},{16,18},{18,... | collective-permute-start | bytes 393224 | tf_op jit(solution)/shard_map/ppermute | solution.py:18
  68.9 52.2 %reduce-scatter.2.cloned.1.call-start = ((), (), s32[]{:S(2)}) async-start(), calls=%async_computation.2 | async-start | bytes 196608 | tf_op jit(solution)/shard_map/reduce_scatter | solution.py:103
  92.4 1.6 %collective-permute-start.6 = (bf16[128,512]{1,0:T(8,128)(2,1)}, bf16[128,512]{1,0:T(8,128)(2,1)S(1)}, u32[]{:S(2)}, u32[]{:S(2)}) collective-permute-start(bf16[128,512]{1,0:T(8,128)(2,1)} %all-reduce.2.cloned.1.call-done), channel_id=1, source_target_pairs={{0,2},{2,0},{4,6},{6,4},{8,10},{10,8},{12,14},{14,12},{16,18},{18,... | collective-permute-start | bytes 393224 | tf_op jit(solution)/shard_map/ppermute | solution.py:18
  92.4 14.5 %collective-permute-start.9 = (bf16[512,512]{1,0:T(8,128)(2,1)}, bf16[512,512]{1,0:T(8,128)(2,1)S(1)}, u32[]{:S(2)}, u32[]{:S(2)}) collective-permute-start(bf16[512,512]{1,0:T(8,128)(2,1)} %collective-permute-done.5), channel_id=1, source_target_pairs={{0,8},{8,0},{2,10},{10,2},{4,12},{12,4},{6,14},{14,6},{16,24},{24,... | collective-permute-start | bytes 1572872 | tf_op jit(solution)/shard_map/ppermute | solution.py:18
  93.9 5.6 %collective-permute-start.7 = (bf16[128,512]{1,0:T(8,128)(2,1)S(1)}, bf16[128,512]{1,0:T(8,128)(2,1)S(1)}, u32[]{:S(2)}, u32[]{:S(2)}) collective-permute-start(bf16[128,512]{1,0:T(8,128)(2,1)S(1)} %broadcast_select_fusion.4), channel_id=1, source_target_pairs={{0,4},{4,0},{2,6},{6,2},{8,12},{12,8},{10,14},{14,10},{16,20},{20,... | collective-permute-start | bytes 393224 | tf_op jit(solution)/shard_map/ppermute | solution.py:18
  102.2 5.5 %collective-permute-start.8 = (bf16[128,512]{1,0:T(8,128)(2,1)}, bf16[128,512]{1,0:T(8,128)(2,1)S(1)}, u32[]{:S(2)}, u32[]{:S(2)}) collective-permute-start(bf16[128,512]{1,0:T(8,128)(2,1)} %get-tuple-element.42), channel_id=1, source_target_pairs={{0,2},{2,0},{4,6},{6,4},{8,10},{10,8},{12,14},{14,12},{16,18},{18,... | collective-permute-start | bytes 393224 | tf_op jit(solution)/shard_map/ppermute | solution.py:18
Sparse Core Ops, SparseCore 0:
  69.0 23.3 all-reduce.1
  110.7 10.2 reduce-scatter.1
where the time goes:
time: 130 us; the launch traced here: 129 us
  waiting for transfers between devices  82.8 us (64%)
  between operations  18.7 us (14%)
  other arithmetic  11.3 us (9%)
  starting transfers between devices  11.2 us (9%)
  matrix products  4.1 us (3%)
    ppermute x10, waiting for transfers between devices, from_partner(): return lax.ppermute(block, axis, route)  48.9 us
    psum x1, waiting for transfers between devices, shards(): squared = lax.psum(partial_value.astype(jnp.bfloat16), 'layer')  23.5 us
    ppermute x10, starting transfers between devices, from_partner(): return lax.ppermute(block, axis, route)  11.1 us
    reduce_scatter x1, waiting for transfers between devices, shards(): lax.psum_scatter(partial_next.astype(jnp.bfloat16), 'layer', scatter_dime...  10.4 us
    reduce_or x7, other arithmetic, tile_product(): occupied = jnp.any(left != 0) & jnp.any(right != 0)  7.63 us
    dot_general x4, matrix products, multiply(): return jnp.dot(operands[0], operands[1], preferred_element_type=jnp.float32)  4.1 us
  transfers between devices with their start and end apart: 12, of which 10 were waited for; matrix products, arithmetic and copies ran while one was open for 6% of the time, Pallas kernels for 0%

commit v1 on v0

v1 whole, which is shorter than its diff:
```python
import functools
import math

import jax
import jax.numpy as jnp
from jax import lax
from jax.experimental import pallas as pl
from jax.experimental.pallas import tpu as pltpu
from jax.sharding import PartitionSpec as P

SLAB = 128
MESH = pl.DeviceIdType.MESH


def flip(number, level):
    step = 1 << level
    return number + (1 - 2 * (number // step % 2)) * step


def nearest(n, a, k):
    inner = jnp.minimum(a, n - 1 - a)
    around = a + (k + 1) // 2 if k % 2 else a - k // 2
    beyond = jnp.where(2 * a < n, k, n - 1 - k)
    return jnp.where(k <= 2 * inner, around, beyond)


def kernel(n, x_ref, pattern_ref, out_ref, own_x, x, m, s, kept, core_out, core_in, far_out, far_in,
           squared, cubed, back_out, back_in, load_sem, s_send, s_recv, core_send, core_recv,
           far_send, far_recv, pair_send, pair_recv, back_send, back_recv):
    position = lax.axis_index("grid")
    a, b = position // n, position % n
    layer = lax.axis_index("layer")
    bits = n.bit_length() - 1
    rows, width = own_x.shape
    half = rows // 2
    blocks = pattern_ref.shape[1]
    span = width // blocks
    core = b % 2
    line = [nearest(n, a, k) for k in range(n)]
    column = [{"grid": line[k] * n + b} for k in range(n)]
    partner = [{"grid": a * n + flip(b, level)} for level in range(bits)]

    barrier = pltpu.get_barrier_semaphore()
    for peer in column[1:] + partner:
        pl.semaphore_signal(barrier, inc=1, device_id=peer, device_id_type=MESH)
    load_own = pltpu.make_async_copy(
        x_ref.at[0, pl.ds(pl.multiple_of(layer * rows, rows), rows), :], own_x, load_sem.at[0])
    load_own.start()
    load_all = pltpu.make_async_copy(x_ref.at[0], x, load_sem.at[1])
    load_all.start()

    def inside(place, block):
        return ((place >= block * span) & (place < (block + 1) * span)).astype(jnp.float32)

    def iota(shape, dim):
        return lax.broadcasted_iota(jnp.int32, shape, dim)

    spread = inside(iota((blocks, width), 1), iota((blocks, width), 0))
    across = jnp.dot(pattern_ref[0].astype(jnp.float32), spread, preferred_element_type=jnp.float32)
    down = inside(iota((rows, blocks), 0) + layer * rows, iota((rows, blocks), 1))
    own_mask = jnp.dot(down, across, preferred_element_type=jnp.float32)
    load_own.wait()
    s[a] = own_x[...] * own_mask.astype(jnp.bfloat16)
    pl.semaphore_wait(barrier, n - 1 + bits)

    def s_copy(k, slot):
        return pltpu.make_async_remote_copy(
            src_ref=s.at[slot], dst_ref=s.at[slot], send_sem=s_send.at[k], recv_sem=s_recv.at[slot],
            device_id=column[k], device_id_type=MESH)

    def core_copy(k):
        return pltpu.make_async_remote_copy(
            src_ref=core_out.at[k], dst_ref=core_in.at[k], send_sem=core_send.at[k],
            recv_sem=core_recv.at[k], device_id=partner[0], device_id_type=MESH)

    def far_copy(k, level):
        return pltpu.make_async_remote_copy(
            src_ref=far_out.at[level - 1, k], dst_ref=far_in.at[level - 1, k],
            send_sem=far_send.at[level - 1, k], recv_sem=far_recv.at[level - 1, k],
            device_id=partner[level], device_id_type=MESH)

    def pair_copy(k, which):
        return pltpu.make_async_remote_copy(
            src_ref=squared.at[k, which], dst_ref=squared.at[k, which], send_sem=pair_send.at[k],
            recv_sem=pair_recv.at[k], device_id=partner[0], device_id_type=MESH)

    def back_copy(k, slot):
        return pltpu.make_async_remote_copy(
            src_ref=back_out.at[k], dst_ref=back_in.at[slot], send_sem=back_send.at[k],
            recv_sem=back_recv.at[slot], device_id=column[k], device_id_type=MESH)

    for k in range(1, n):
        s_copy(k, a).start()
    load_all.wait()
    for block in range(blocks):
        part = pl.ds(block * span, span)
        m[part, :] = x[part, :] * across[block:block + 1, :].astype(jnp.bfloat16)

    def first(k):
        if k > 0:
            s_copy(k, line[k]).wait_recv()
        product = lax.dot_general(
            s[line[k]], m[...], (((1,), (1,)), ((), ())), preferred_element_type=jnp.float32)
        low, high = product[:half], product[half:]
        core_out[k] = jnp.where(core == 0, high, low).astype(jnp.bfloat16)
        core_copy(k).start()
        kept[k] = jnp.where(core == 0, low, high)

    def pair_sum(k):
        core_copy(k).wait_recv()
        total = kept[k] + core_in[k].astype(jnp.float32)
        kept[k] = total
        far_out[0, k] = total.astype(jnp.bfloat16)
        far_copy(k, 1).start()

    def row_sum(k):
        for level in range(1, bits):
            far_copy(k, level).wait_recv()
            total = kept[k] + far_in[level - 1, k].astype(jnp.float32)
            if level + 1 < bits:
                kept[k] = total
                far_out[level, k] = total.astype(jnp.bfloat16)
                far_copy(k, level + 1).start()
        squared[k, core] = total.astype(jnp.bfloat16)
        pair_copy(k, core).start()

    def second(k):
        pair_copy(k, 1 - core).wait_recv()
        left = squared[k].reshape(rows, width)
        product = jnp.dot(left, m[...], preferred_element_type=jnp.float32)
        if k == 0:
            cubed[...] = product
        else:
            back_out[k] = product.astype(jnp.bfloat16)
            back_copy(k, a).start()

    stages = [second, row_sum, pair_sum, first]
    for turn in range(n + 3):
        for late, stage in enumerate(stages):
            k = turn - 3 + late
            if 0 <= k < n:
                stage(k)

    total = cubed[...]
    for k in range(1, n):
        back_copy(k, line[k]).wait_recv()
        total = total + back_in[line[k]].astype(jnp.float32)
    out_ref[0] = (1.5 * s[a].astype(jnp.float32) - 0.5 * total).astype(jnp.bfloat16)
    for k in range(n):
        core_copy(k).wait_send()
        for level in range(1, bits):
            far_copy(k, level).wait_send()
        pair_copy(k, core).wait_send()
        if k > 0:
            s_copy(k, a).wait_send()
            back_copy(k, a).wait_send()


def shards(x_tiles, pattern):
    n = math.isqrt(lax.axis_size("grid"))
    bits = n.bit_length() - 1
    rows = SLAB // lax.axis_size("layer")
    width = x_tiles.shape[2]
    half = rows // 2
    bf16, f32 = jnp.bfloat16, jnp.float32
    dma = pltpu.SemaphoreType.DMA
    return pl.pallas_call(
        functools.partial(kernel, n),
        out_shape=jax.ShapeDtypeStruct((1, rows, width), bf16),
        in_specs=[pl.BlockSpec(memory_space=pl.ANY), pl.BlockSpec(memory_space=pltpu.VMEM)],
        out_specs=pl.BlockSpec(memory_space=pltpu.VMEM),
        scratch_shapes=[
            pltpu.VMEM((rows, width), bf16),
            pltpu.VMEM((width, width), bf16),
            pltpu.VMEM((width, width), bf16),
            pltpu.VMEM((n, rows, width), bf16),
            pltpu.VMEM((n, half, width), f32),
            pltpu.VMEM((n, half, width), bf16),
            pltpu.VMEM((n, half, width), bf16),
            pltpu.VMEM((bits - 1, n, half, width), bf16),
            pltpu.VMEM((bits - 1, n, half, width), bf16),
            pltpu.VMEM((n, 2, half, width), bf16),
            pltpu.VMEM((rows, width), f32),
            pltpu.VMEM((n, rows, width), bf16),
            pltpu.VMEM((n, rows, width), bf16),
            dma((2,)),
            dma((n,)), dma((n,)),
            dma((n,)), dma((n,)),
            dma((bits - 1, n)), dma((bits - 1, n)),
            dma((n,)), dma((n,)),
            dma((n,)), dma((n,)),
        ],
        compiler_params=pltpu.CompilerParams(
            collective_id=0, has_side_effects=True, vmem_limit_bytes=40 * 1024 * 1024),
        cost_estimate=pl.CostEstimate(
            flops=4 * n * rows * width * width, bytes_accessed=2 * width * width, transcendentals=0),
    )(x_tiles, pattern)


def solution(mesh):
    in_specs = (P("grid", None, None), P("grid", None, None))
    out_specs = P("grid", "layer", None)
    return jax.shard_map(shards, mesh=mesh, in_specs=in_specs, out_specs=out_specs, check_vma=False)
```

time: 130 us -> 27.4 us (0.21)
  waiting for transfers between devices: 82.8 us -> 0 us
  Pallas kernels: 0 us -> 24.8 us
  between operations: 18.7 us -> 0.01 us
  other arithmetic: 11.3 us -> 0 us
  starting transfers between devices: 11.2 us -> 0 us
  matrix products: 4.1 us -> 0 us
    ppermute x10 -> x0, waiting for transfers between devices: 48.9 us -> none  [from_partner(): return lax.ppermute(block, axis, route)]
    pallas_call x0 -> x1, Pallas kernels: none -> 24.8 us  [shards(): pl.pallas_call(functools.partial(kernel, n), out_shape=jax.ShapeDtypeStru...]
    psum x1 -> x0, waiting for transfers between devices: 23.5 us -> none  [shards(): squared = lax.psum(partial_value.astype(jnp.bfloat16), 'layer')]
    ppermute x10 -> x0, starting transfers between devices: 11.1 us -> none  [from_partner(): return lax.ppermute(block, axis, route)]
    reduce_scatter x1 -> x0, waiting for transfers between devices: 10.4 us -> none  [shards(): lax.psum_scatter(partial_next.astype(jnp.bfloat16), 'layer', scatter_dime...]
    reduce_or x7 -> x0, other arithmetic: 7.63 us -> none  [tile_product(): occupied = jnp.any(left != 0) & jnp.any(right != 0)]
    dot_general x4 -> x0, matrix products: 4.1 us -> none  [multiply(): return jnp.dot(operands[0], operands[1], preferred_element_type=jnp.float32)]
    convert_element_type x3 -> x0, other arithmetic: 2.05 us -> none  [the longest x1 0.69 us: shards(): mask = mask.reshape(width, width).astype(jnp.bfloat16)]
  transfers between devices with their start and end apart: 12 -> 0, of which waited for: 10 -> 0; matrix products, arithmetic and copies ran while one was open for 6% -> 0% of each run, Pallas kernels for 0% -> 0%
where the time goes in v1:
time: 27.4 us; the launch traced here: 27.2 us
  Pallas kernels  24.8 us (91%)
  local copies, waits for them, and re-layouts  2.36 us (9%)
    pallas_call x1, Pallas kernels, shards(): pl.pallas_call(functools.partial(kernel, n), out_shape=jax.ShapeDtypeStru...  24.8 us
    unnamed x5, local copies, waits for them, and re-layouts  2.36 us

profile of v1, /device:TPU:0, one launch (start us, length us, event | category | flops | bytes accessed | tf_op | source)
XLA Modules:
  0.0 27.2 jit_solution(295222124168122391)
XLA Ops:
  0.0 0.0 copy-start
  0.0 1.0 %copy-done = bf16[1,512,512]{2,1,0:T(8,128)(2,1)S(1)} copy-done((bf16[1,512,512]{2,1,0:T(8,128)(2,1)S(1)}, bf16[1,512,512]{2,1,0:T(8,128)(2,1)}, u32[]{:S(2)}) %copy-start) | copy-done | bytes 524312
  1.0 0.0 copy-start.1
  1.0 0.7 %copy-done.1 = s32[1,8,8]{2,1,0:T(8,128)S(1)} copy-done((s32[1,8,8]{2,1,0:T(8,128)S(1)}, s32[1,8,8]{2,1,0:T(8,128)}, u32[]{:S(2)}) %copy-start.1) | copy-done | bytes 280
  1.7 24.8 %shard_map.28 = bf16[1,64,512]{2,1,0:T(8,128)(2,1)S(1)} custom-call(bf16[1,512,512]{2,1,0:T(8,128)(2,1)S(1)} %copy-done, s32[1,8,8]{2,1,0:T(8,128)S(1)} %copy-done.1), custom_call_target="tpu_custom_call" | custom-call | flops 268435456 | bytes 524288 | tf_op jit(solution)/shard_map/pallas_call | solution.py:167
  26.5 0.6 %copy.4 = bf16[1,64,512]{2,1,0:T(8,128)(2,1)} copy(bf16[1,64,512]{2,1,0:T(8,128)(2,1)S(1)} %shard_map.28) | data formatting | bytes 131072
Async XLA Ops:
  0.0 1.0 %copy-start = (bf16[1,512,512]{2,1,0:T(8,128)(2,1)S(1)}, bf16[1,512,512]{2,1,0:T(8,128)(2,1)}, u32[]{:S(2)}) copy-start(bf16[1,512,512]{2,1,0:T(8,128)(2,1)} %x_ref.1) | copy-start | bytes 1572868
  1.0 0.7 %copy-start.1 = (s32[1,8,8]{2,1,0:T(8,128)S(1)}, s32[1,8,8]{2,1,0:T(8,128)}, u32[]{:S(2)}) copy-start(s32[1,8,8]{2,1,0:T(8,128)} %pattern_ref.1) | copy-start | bytes 772

commit v2 on v1

v2 whole, which is shorter than its diff:
```python
import functools
import math

import jax
import jax.numpy as jnp
from jax import lax
from jax.experimental import pallas as pl
from jax.experimental.pallas import tpu as pltpu
from jax.sharding import PartitionSpec as P

SLAB = 128
MESH = pl.DeviceIdType.MESH


def flip(number, level):
    step = 1 << level
    return number + (1 - 2 * (number // step % 2)) * step


def xor(number, mask):
    for level in range(mask.bit_length()):
        if mask >> level & 1:
            number = flip(number, level)
    return number


def kernel(n, x_ref, pattern_ref, out_ref, pattern, own_x, x, m, s, kept, core_out, core_in, far_out,
           far_in, cubed, back_out, back_in, load_sem, s_send, s_recv, core_send, core_recv,
           far_send, far_recv, back_send, back_recv):
    position = lax.axis_index("grid")
    a, b = position // n, position % n
    layer = lax.axis_index("layer")
    bits = n.bit_length() - 1
    rows, width = own_x.shape
    half = rows // 2
    blocks = pattern.shape[1]
    span = width // blocks
    core = b % 2
    order = [0, 1] + [k ^ 1 for k in range(2, n)]
    line = [xor(a, k) for k in order]
    column = [{"grid": line[k] * n + b} for k in range(n)]
    partner = [a * n + flip(b, level) for level in range(bits)]
    across_chips = [(level, other) for level in range(1, bits) for other in range(2)]
    row = [{"grid": partner[0]}]
    for level, other in across_chips:
        row.append({"grid": partner[level] if other == 0 else flip(partner[level], 0)})

    barrier = pltpu.get_barrier_semaphore()
    for peer in column[1:] + row:
        pl.semaphore_signal(barrier, inc=1, device_id=peer, device_id_type=MESH)
    load_pattern = pltpu.make_async_copy(pattern_ref, pattern, load_sem.at[2])
    load_pattern.start()
    load_own = pltpu.make_async_copy(
        x_ref.at[0, pl.ds(pl.multiple_of(layer * rows, rows), rows), :], own_x, load_sem.at[0])
    load_own.start()
    load_all = pltpu.make_async_copy(x_ref.at[0], x, load_sem.at[1])
    load_all.start()

    def inside(place, block):
        return ((place >= block * span) & (place < (block + 1) * span)).astype(jnp.float32)

    def iota(shape, dim):
        return lax.broadcasted_iota(jnp.int32, shape, dim)

    spread = inside(iota((blocks, width), 1), iota((blocks, width), 0))
    load_pattern.wait()
    across = jnp.dot(pattern[0].astype(jnp.float32), spread, preferred_element_type=jnp.float32)
    down = inside(iota((rows, blocks), 0) + layer * rows, iota((rows, blocks), 1))
    own_mask = jnp.dot(down, across, preferred_element_type=jnp.float32)
    load_own.wait()
    s[a] = own_x[...] * own_mask.astype(jnp.bfloat16)
    pl.semaphore_wait(barrier, n - 1 + len(row))

    def s_copy(k, slot):
        return pltpu.make_async_remote_copy(
            src_ref=s.at[slot], dst_ref=s.at[slot], send_sem=s_send.at[k], recv_sem=s_recv.at[slot],
            device_id=column[k], device_id_type=MESH)

    def core_copy(k):
        return pltpu.make_async_remote_copy(
            src_ref=core_out.at[k], dst_ref=core_in.at[k], send_sem=core_send.at[k],
            recv_sem=core_recv.at[k], device_id=row[0], device_id_type=MESH)

    def far_copy(k, level, other, which):
        return pltpu.make_async_remote_copy(
            src_ref=far_out.at[level - 1, k], dst_ref=far_in.at[level - 1, k, which],
            send_sem=far_send.at[level - 1, k, other], recv_sem=far_recv.at[level - 1, k, which],
            device_id=row[2 * level - 1 + other], device_id_type=MESH)

    def back_copy(k, slot):
        return pltpu.make_async_remote_copy(
            src_ref=back_out.at[k], dst_ref=back_in.at[slot], send_sem=back_send.at[k],
            recv_sem=back_recv.at[slot], device_id=column[k], device_id_type=MESH)

    for k in range(1, n):
        s_copy(k, a).start()
    load_all.wait()
    for block in range(blocks):
        part = pl.ds(block * span, span)
        m[part, :] = x[part, :] * across[block:block + 1, :].astype(jnp.bfloat16)

    def first(k):
        if k > 0:
            s_copy(k, line[k]).wait_recv()
        product = lax.dot_general(
            s[line[k]], m[...], (((1,), (1,)), ((), ())), preferred_element_type=jnp.float32)
        core_out[k] = product.astype(jnp.bfloat16)
        core_copy(k).start()
        kept[k] = product

    def send_half(k, level, total):
        far_out[level - 1, k] = jnp.where(core == 0, total[:half], total[half:]).astype(jnp.bfloat16)
        for other in range(2):
            far_copy(k, level, other, core).start()

    def pair_sum(k):
        core_copy(k).wait_recv()
        total = kept[k] + core_in[k].astype(jnp.float32)
        kept[k] = total
        send_half(k, 1, total)

    def second(k):
        total = kept[k]
        for level in range(1, bits):
            for which in range(2):
                far_copy(k, level, 0, which).wait_recv()
            total = total + far_in[level - 1, k].reshape(rows, width).astype(jnp.float32)
            if level + 1 < bits:
                send_half(k, level + 1, total)
        product = jnp.dot(total.astype(jnp.bfloat16), m[...], preferred_element_type=jnp.float32)
        if k == 0:
            cubed[...] = product
        else:
            back_out[k] = product.astype(jnp.bfloat16)
            back_copy(k, a).start()

    for k in range(n):
        first(k)
        pair_sum(k)
    for k in range(n):
        second(k)

    total = cubed[...]
    for k in range(1, n):
        back_copy(k, line[k]).wait_recv()
        total = total + back_in[line[k]].astype(jnp.float32)
    out_ref[0] = (1.5 * s[a].astype(jnp.float32) - 0.5 * total).astype(jnp.bfloat16)
    for k in range(n):
        core_copy(k).wait_send()
        for level, other in across_chips:
            far_copy(k, level, other, core).wait_send()
        if k > 0:
            s_copy(k, a).wait_send()
            back_copy(k, a).wait_send()


def shards(x_tiles, pattern):
    n = math.isqrt(lax.axis_size("grid"))
    bits = n.bit_length() - 1
    rows = SLAB // lax.axis_size("layer")
    width = x_tiles.shape[2]
    half = rows // 2
    bf16, f32 = jnp.bfloat16, jnp.float32
    dma = pltpu.SemaphoreType.DMA
    return pl.pallas_call(
        functools.partial(kernel, n),
        out_shape=jax.ShapeDtypeStruct((1, rows, width), bf16),
        in_specs=[pl.BlockSpec(memory_space=pltpu.HBM)] * 2,
        out_specs=pl.BlockSpec(memory_space=pltpu.VMEM),
        scratch_shapes=[
            pltpu.VMEM(pattern.shape, pattern.dtype),
            pltpu.VMEM((rows, width), bf16),
            pltpu.VMEM((width, width), bf16),
            pltpu.VMEM((width, width), bf16),
            pltpu.VMEM((n, rows, width), bf16),
            pltpu.VMEM((n, rows, width), f32),
            pltpu.VMEM((n, rows, width), bf16),
            pltpu.VMEM((n, rows, width), bf16),
            pltpu.VMEM((bits - 1, n, half, width), bf16),
            pltpu.VMEM((bits - 1, n, 2, half, width), bf16),
            pltpu.VMEM((rows, width), f32),
            pltpu.VMEM((n, rows, width), bf16),
            pltpu.VMEM((n, rows, width), bf16),
            dma((3,)),
            dma((n,)), dma((n,)),
            dma((n,)), dma((n,)),
            dma((bits - 1, n, 2)), dma((bits - 1, n, 2)),
            dma((n,)), dma((n,)),
        ],
        compiler_params=pltpu.CompilerParams(
            collective_id=0, has_side_effects=True, vmem_limit_bytes=63 * 1024 * 1024),
        cost_estimate=pl.CostEstimate(
            flops=4 * n * rows * width * width, bytes_accessed=2 * width * width, transcendentals=0),
    )(x_tiles, pattern)


def solution(mesh):
    in_specs = (P("grid", None, None), P("grid", None, None))
    out_specs = P("grid", "layer", None)
    return jax.shard_map(shards, mesh=mesh, in_specs=in_specs, out_specs=out_specs, check_vma=False)
```

time: 27.4 us -> 25.1 us (0.916)
  Pallas kernels: 24.8 us -> 23.5 us
  local copies, waits for them, and re-layouts: 2.36 us -> 1.47 us
    pallas_call x1, Pallas kernels: 24.8 us -> 23.5 us  [shards(): pl.pallas_call(functools.partial(kernel, n), out_shape=jax.ShapeDtypeStru...]
    unnamed x5 -> x1, local copies, waits for them, and re-layouts: 2.36 us -> 1.47 us
where the time goes in v2:
time: 25.1 us; the launch traced here: 25 us
  Pallas kernels  23.5 us (94%)
  local copies, waits for them, and re-layouts  1.47 us (6%)
    pallas_call x1, Pallas kernels, shards(): pl.pallas_call(functools.partial(kernel, n), out_shape=jax.ShapeDtypeStru...  23.5 us
    unnamed x1, local copies, waits for them, and re-layouts  1.47 us

profile of v2, /device:TPU:0, one launch (start us, length us, event | category | flops | bytes accessed | tf_op | source)
XLA Modules:
  0.0 25.0 jit_solution(15247620933645041516)
XLA Ops:
  0.0 23.5 %shard_map.28 = bf16[1,64,512]{2,1,0:T(8,128)(2,1)} custom-call(bf16[1,512,512]{2,1,0:T(8,128)(2,1)} %x_ref.1, s32[1,8,8]{2,1,0:T(8,128)} %pattern_ref.1), custom_call_target="tpu_custom_call" | custom-call | flops 268435456 | bytes 524288 | tf_op jit(solution)/shard_map/pallas_call | solution.py:165
  23.5 1.5 %copy.4 = bf16[1,64,512]{2,1,0:T(8,128)(2,1)} copy(bf16[1,64,512]{2,1,0:T(8,128)(2,1)} %shard_map.28) | data formatting | bytes 131072

commit v3 on v2

--- a/solution.py
+++ b/solution.py
@@ -36,8 +36,7 @@
     blocks = pattern.shape[1]
     span = width // blocks
     core = b % 2
-    order = [0, 1] + [k ^ 1 for k in range(2, n)]
-    line = [xor(a, k) for k in order]
+    line = [xor(a, k) for k in range(n)]
     column = [{"grid": line[k] * n + b} for k in range(n)]
     partner = [a * n + flip(b, level) for level in range(bits)]
     across_chips = [(level, other) for level in range(1, bits) for other in range(2)]
@@ -137,7 +136,7 @@
     for k in range(n):
         first(k)
         pair_sum(k)
-    for k in range(n):
+    for k in [*range(1, n - 1), 0, n - 1]:
         second(k)
 
     total = cubed[...]

time: 25.1 us -> 24.7 us (0.984)
  Pallas kernels: 23.5 us -> 23 us
    pallas_call x1, Pallas kernels: 23.5 us -> 23 us  [shards(): pl.pallas_call(functools.partial(kernel, n), out_shape=jax.ShapeDtypeStru...]
where the time goes in v3:
time: 24.7 us; the launch traced here: 24.5 us
  Pallas kernels  23 us (93%)
  local copies, waits for them, and re-layouts  1.47 us (6%)
    pallas_call x1, Pallas kernels, shards(): pl.pallas_call(functools.partial(kernel, n), out_shape=jax.ShapeDtypeStru...  23 us
    unnamed x1, local copies, waits for them, and re-layouts  1.47 us

profile of v3, /device:TPU:0, one launch (start us, length us, event | category | flops | bytes accessed | tf_op | source)
XLA Modules:
  0.0 24.5 jit_solution(12754636520692325536)
XLA Ops:
  0.0 23.0 %shard_map.28 = bf16[1,64,512]{2,1,0:T(8,128)(2,1)} custom-call(bf16[1,512,512]{2,1,0:T(8,128)(2,1)} %x_ref.1, s32[1,8,8]{2,1,0:T(8,128)} %pattern_ref.1), custom_call_target="tpu_custom_call" | custom-call | flops 268435456 | bytes 524288 | tf_op jit(solution)/shard_map/pallas_call | solution.py:164
  23.0 1.5 %copy.4 = bf16[1,64,512]{2,1,0:T(8,128)(2,1)} copy(bf16[1,64,512]{2,1,0:T(8,128)(2,1)} %shard_map.28) | data formatting | bytes 131072
